TPU v7x, 128 devices: a whole 4x4x4 slice. The times are simulated.
128 devices in a mesh: dp: 8 (over x, z_hi), tensor: 16 (over y, z_lo, core).
Axes of the slice: x: 4, y: 4, z: 4 (z_hi: 2, z_lo: 2; z = z_hi * 2 + z_lo), core: 2. Of those that a mesh axis runs over, the one named last changes fastest.
Arguments:
- out_grads: bfloat16 [32768, 4096], P('dp', 'tensor'), may hold values from -6 to 6
- inputs: bfloat16 [32768, 1024], P('dp', 'tensor'), may hold values from -6 to 6
- out_proj: bfloat16 [4096, 2048], P('tensor'), may hold values from -0.09375 to 0.09375
- in_proj: bfloat16 [1024, 2048], P('tensor'), may hold values from -0.1875 to 0.1875
- prev_gram: float32 [2048, 2048], P('tensor'), may hold values from -3 to 3
Outputs:
- features: float32 [64, 2048], P('dp', 'tensor')
- gram: float32 [2048, 2048], P('tensor')
All inputs are finite; a program needn't handle non-finite values.
Results may differ from a plain program's by a relative error of at most 0.0003.
Values may be sent and summed in bfloat16 or wider, within the bound.
A program may use at most 256 MiB of HBM per device.

v0:
```python
import math

import jax
import jax.numpy as jnp
from jax import lax
from jax.sharding import PartitionSpec as P

SEQ = 512


def clip_features(products, own_rows, clip_count):
    first_token = lax.axis_index("tensor") * own_rows
    token_index = first_token + lax.iota(jnp.int32, own_rows)
    clip_index = token_index // SEQ
    membership = (clip_index[None, :] == lax.iota(jnp.int32, clip_count)[:, None]).astype(
        jnp.float32
    )
    partial_value = jnp.dot(
        membership, products, precision=lax.Precision.HIGHEST, preferred_element_type=jnp.float32
    )
    return lax.psum(partial_value, "tensor")


def local(out_grads, inputs, out_proj, in_proj, prev_gram):
    tensor_count = lax.axis_size("tensor")
    row_count = out_grads.shape[0]
    proj_width = out_proj.shape[1]
    clip_count = row_count // SEQ
    own_width = proj_width // tensor_count
    own_rows = row_count // tensor_count
    norm_scale = jnp.float32(1.0 / math.sqrt(SEQ))
    out_part = jnp.dot(out_grads, out_proj, preferred_element_type=jnp.float32)
    in_part = jnp.dot(inputs, in_proj, preferred_element_type=jnp.float32)
    shared_sums = lax.psum_scatter(
        jnp.concatenate([out_part, in_part], axis=1), "tensor", scatter_dimension=0, tiled=True
    )
    products = shared_sums[:, :proj_width] * shared_sums[:, proj_width:]
    features = clip_features(products, own_rows, clip_count) * norm_scale
    own_features = lax.dynamic_slice_in_dim(
        features, lax.axis_index("tensor") * own_width, own_width, 1
    )
    gram_part = jnp.dot(
        own_features.T,
        features,
        precision=lax.Precision.HIGHEST,
        preferred_element_type=jnp.float32,
    )
    gram_total = lax.psum(gram_part, "dp")
    gram = prev_gram + gram_total / jnp.float32(clip_count * lax.axis_size("dp"))
    return (own_features, gram)


def solution(mesh):
    return jax.shard_map(
        local,
        mesh=mesh,
        in_specs=(
            P("dp", "tensor"),
            P("dp", "tensor"),
            P("tensor", None),
            P("tensor", None),
            P("tensor", None),
        ),
        out_specs=(P("dp", "tensor"), P("tensor", None)),
        check_vma=False,
    )
```

profile of v0, /device:TPU:1, one launch (start us, length us, event | category | flops | bytes accessed | tf_op | source)
XLA Modules:
  0.0 976.3 jit_solution(18384837904111256000)
XLA Ops:
  7.2 0.0 copy-start
  7.2 0.0 copy-start.2
  7.2 0.0 reduce-scatter.2.cloned.1.call-start
  7.2 16.9 %fusion.5 = f32[4096,2048]{0,1:T(8,128)} fusion(bf16[4096,64]{0,1:T(8,128)(2,1)} %param.6, bf16[64,2048]{1,0:T(8,128)(2,1)} %param.8), kind=kOutput, calls=%fused_computation.15 | convolution fusion | flops 1073741824 | bytes 34340864 | tf_op jit(solution)/shard_map/dot_general | solution.py:33
  24.1 0.0 copy-done
  24.1 0.0 copy-done.2
  24.1 13.1 %fusion.4 = f32[4096,2048]{0,1:T(8,128)} fusion(bf16[4096,256]{1,0:T(8,128)(2,1)S(1)} %copy-done, bf16[256,2048]{1,0:T(8,128)(2,1)S(1)} %copy-done.2), kind=kOutput, calls=%fused_computation.14 | convolution fusion | flops 4294967296 | bytes 36700160 | tf_op jit(solution)/shard_map/dot_general | solution.py:32
  37.2 44.0 %pad_maximum_fusion = f32[4096,4096]{0,1:T(8,128)} fusion(f32[4096,2048]{0,1:T(8,128)} %fusion.5, f32[4096,2048]{0,1:T(8,128)} %fusion.4), kind=kLoop, calls=%fused_computation | loop fusion | flops 16777216 | bytes 134217728 | tf_op jit(solution)/shard_map/concatenate | solution.py:35
  81.2 0.0 reduce-scatter.2.cloned.1.call-update
  81.3 0.0 copy-start.3
  81.3 0.0 copy-start.1
  81.3 0.0 all-reduce.3.cloned.1.call-start
  81.4 689.7 %reduce-scatter.2.cloned.1.call-done = f32[256,4096]{0,1:T(8,128)} async-done(((f32[4096,4096]{0,1:T(8,128)}), f32[256,4096]{0,1:T(8,128)}) %reduce-scatter.2.cloned.1.call-update) | async-done | bytes 4194320 | tf_op jit(solution)/shard_map/reduce_scatter | solution.py:34
  771.0 4.0 fusion
  775.0 0.0 all-reduce.3.cloned.1.call-update
  775.0 0.0 all-reduce.5.cloned.1.call-start
  775.1 104.3 %all-reduce.3.cloned.1.call-done = f32[8,2048]{1,0:T(8,128)} async-done(((f32[8,2048]{1,0:T(8,128)}), f32[8,2048]{1,0:T(8,128)}) %all-reduce.3.cloned.1.call-update) | async-done | bytes 65552 | tf_op jit(solution)/shard_map/psum | solution.py:21
  879.4 0.8 broadcast_multiply_fusion
  880.2 0.0 copy-start.4
  880.2 2.8 fusion.3
  883.1 0.0 all-reduce.5.cloned.1.call-update
  883.1 84.4 %all-reduce.5.cloned.1.call-done = f32[128,2048]{1,0:T(8,128)} async-done(((f32[128,2048]{1,0:T(8,128)}), f32[128,2048]{1,0:T(8,128)}) %all-reduce.5.cloned.1.call-update) | async-done | bytes 1048592 | tf_op jit(solution)/shard_map/psum | solution.py:48
  967.5 0.0 copy-done.3
  967.5 2.3 multiply_add_fusion
  969.8 0.0 copy-done.4
  969.8 0.0 copy-done.1
  (2 shorter events, 0.0 us)
Async XLA Ops:
  7.2 16.9 %copy-start = (bf16[4096,256]{1,0:T(8,128)(2,1)S(1)}, bf16[4096,256]{1,0:T(8,128)(2,1)}, u32[]{:S(2)}) copy-start(bf16[4096,256]{1,0:T(8,128)(2,1)} %param.5) | copy-start | bytes 6291460
  7.2 16.9 %copy-start.2 = (bf16[256,2048]{1,0:T(8,128)(2,1)S(1)}, bf16[256,2048]{1,0:T(8,128)(2,1)}, u32[]{:S(2)}) copy-start(bf16[256,2048]{1,0:T(8,128)(2,1)} %param.7) | copy-start | bytes 3145732
  7.2 763.9 %reduce-scatter.2.cloned.1.call-start = ((), (), s32[]{:S(2)}) async-start(), calls=%async_computation.1 | async-start | bytes 71303168 | tf_op jit(solution)/shard_map/reduce_scatter | solution.py:34
  81.3 886.2 %copy-start.3 = (f32[128,2048]{1,0:T(8,128)S(1)}, f32[128,2048]{1,0:T(8,128)}, u32[]{:S(2)}) copy-start(f32[128,2048]{1,0:T(8,128)} %param.9) | copy-start | bytes 3145732
  81.3 888.5 %copy-start.1 = (bf16[4096,256]{1,0:T(8,128)(2,1)S(1)}, bf16[4096,256]{1,0:T(8,128)(2,1)}, u32[]{:S(2)}) copy-start(bf16[4096,256]{1,0:T(8,128)(2,1)} %param.5) | copy-start | bytes 6291460
  81.3 798.1 %all-reduce.3.cloned.1.call-start = ((), (), s32[]{:S(2)}) async-start(), calls=%async_computation.2 | async-start | bytes 131072 | tf_op jit(solution)/shard_map/psum | solution.py:21
  775.0 192.4 %all-reduce.5.cloned.1.call-start = ((), (), s32[]{:S(2)}) async-start(), calls=%async_computation.3 | async-start | bytes 2097152 | tf_op jit(solution)/shard_map/psum | solution.py:48
  880.2 89.6 %copy-start.4 = (f32[8,128]{1,0:T(8,128)}, f32[8,128]{1,0:T(8,128)S(1)}, u32[]{:S(2)}) copy-start(f32[8,128]{1,0:T(8,128)S(1)} %constant_dynamic-slice_fusion) | copy-start | bytes 12292
Sparse Core Ops, SparseCore 0:
  81.4 689.6 reduce-scatter.1
  775.1 104.1 all-reduce.2
  883.2 84.2 all-reduce.4
where the time goes:
time: 981 us; the launch traced here: 976 us
  waiting for transfers between devices  878 us (90%)
  other arithmetic  47.2 us (5%)
  matrix products  36.7 us (4%)
  between operations  13.8 us (1%)
    reduce_scatter x1, waiting for transfers between devices, local(): lax.psum_scatter(jnp.concatenate([out_part, in_part], axis=1), 'tensor',...  690 us
    psum x1, waiting for transfers between devices, clip_features(): return lax.psum(partial_value, 'tensor')  104 us
    psum x1, waiting for transfers between devices, local(): gram_total = lax.psum(gram_part, 'dp')  84.4 us
    concatenate x1, other arithmetic, local(): jnp.concatenate([out_part, in_part], axis=1)  44 us
  transfers between devices with their start and end apart: 3, of which 3 were waited for; matrix products, arithmetic and copies ran while one was open for 0% of the time, Pallas kernels for 0%

commit v1 on v0

v1 whole, which is shorter than its diff:
```python
import math

import jax
import jax.numpy as jnp
from jax import lax
from jax.sharding import PartitionSpec as P

SEQ = 512


def local(out_grads, inputs, out_proj, in_proj, prev_gram):
    row_count = out_grads.shape[0]
    clip_count = row_count // SEQ
    width = out_proj.shape[1]
    norm_scale = jnp.float32(1.0 / math.sqrt(SEQ))
    all_inputs = lax.all_gather(inputs, "tensor", axis=1, tiled=True)
    all_in_proj = lax.all_gather(in_proj, "tensor", axis=0, tiled=True)
    out_part = jnp.dot(out_grads, out_proj, preferred_element_type=jnp.float32)
    in_side = jnp.dot(all_inputs, all_in_proj, preferred_element_type=jnp.float32)
    partial_features = jnp.sum((out_part * in_side).reshape(clip_count, SEQ, width), axis=1)
    own = lax.psum_scatter(partial_features, "tensor", scatter_dimension=1, tiled=True) * norm_scale
    own_columns = lax.all_gather(own, "dp", axis=0, tiled=True)
    features = lax.all_gather(own_columns, "tensor", axis=1, tiled=True)
    gram_part = jnp.dot(
        own_columns.T,
        features,
        precision=lax.Precision.HIGHEST,
        preferred_element_type=jnp.float32,
    )
    gram = prev_gram + gram_part / jnp.float32(clip_count * lax.axis_size("dp"))
    return (own, gram)


def solution(mesh):
    return jax.shard_map(
        local,
        mesh=mesh,
        in_specs=(
            P("dp", "tensor"),
            P("dp", "tensor"),
            P("tensor", None),
            P("tensor", None),
            P("tensor", None),
        ),
        out_specs=(P("dp", "tensor"), P("tensor", None)),
        check_vma=False,
    )
```

time: 981 us -> 252 us (0.26)
  waiting for transfers between devices: 878 us -> 140 us
  blocking collectives: 0 us -> 55.8 us
  other arithmetic: 47.2 us -> 0.68 us
    reduce_scatter x1, waiting for transfers between devices: 690 us -> 57.1 us  [local(): lax.psum_scatter(partial_features, 'tensor', scatter_dimension=1, tiled=T...]
    psum x2 -> x0, waiting for transfers between devices: 189 us -> none  [the longest x1 104 us: clip_features(): return lax.psum(partial_value, 'tensor')]
    all_gather x0 -> x2, waiting for transfers between devices: none -> 81.5 us  [the longest x1 54 us: local(): all_inputs = lax.all_gather(inputs, 'tensor', axis=1, tiled=True)]
    all_gather x0 -> x2, blocking collectives: none -> 55.8 us  [the longest x1 27.9 us: local(): features = lax.all_gather(own_columns, 'tensor', axis=1, tiled=True)]
    concatenate x1 -> x0, other arithmetic: 44 us -> none  [local(): jnp.concatenate([out_part, in_part], axis=1)]
    dot_general x3 -> x2, matrix products: 23.6 us -> 27.2 us  [the longest x1 25.2 us: local(): jnp.dot(all_inputs, all_in_proj, preferred_element_type=jnp.float32)]
  transfers between devices with their start and end apart: 3 -> 3, of which waited for: 3 -> 3; matrix products, arithmetic and copies ran while one was open for 0% -> 6% of each run, Pallas kernels for 0% -> 0%
where the time goes in v1:
time: 252 us
  waiting for transfers between devices  140 us (56%)
  blocking collectives  55.8 us (22%)
  matrix products  41.7 us (17%)
  between operations  13.8 us (5%)
    reduce_scatter x1, waiting for transfers between devices, local(): lax.psum_scatter(partial_features, 'tensor', scatter_dimension=1, tiled=T...  57.1 us
    all_gather x1, waiting for transfers between devices, local(): all_inputs = lax.all_gather(inputs, 'tensor', axis=1, tiled=True)  54 us
    all_gather x1, blocking collectives, local(): features = lax.all_gather(own_columns, 'tensor', axis=1, tiled=True)  27.9 us
    all_gather x1, blocking collectives, local(): own_columns = lax.all_gather(own, 'dp', axis=0, tiled=True)  27.8 us
    all_gather x1, waiting for transfers between devices, local(): all_in_proj = lax.all_gather(in_proj, 'tensor', axis=0, tiled=True)  27.5 us
    dot_general x1, matrix products, local(): jnp.dot(all_inputs, all_in_proj, preferred_element_type=jnp.float32)  25.2 us
    dot_general x1, matrix products, local(): out_part = jnp.dot(out_grads, out_proj, preferred_element_type=jnp.float32)  14.5 us
  transfers between devices with their start and end apart: 3, of which 3 were waited for; matrix products, arithmetic and copies ran while one was open for 6% of the time, Pallas kernels for 0%

profile of v1, /device:TPU:1, one launch (start us, length us, event | category | flops | bytes accessed | tf_op | source)
XLA Modules:
  0.0 252.0 jit_solution(931667995336053480)
XLA Ops:
  7.2 0.0 copy-start
  7.2 0.0 all-gather.5.cloned.1.call-start
  7.2 0.7 all-gather.5.cloned.1.call-update
  7.9 0.0 all-gather.3.cloned.1.call-start
  8.0 0.7 all-gather.3.cloned.1.call-update
  8.7 0.0 reduce-scatter.2.cloned.1.call-start
  8.7 0.1 copy-done
  8.8 14.5 %fusion.1 = f32[4096,2048]{1,0:T(8,128)} fusion(bf16[4096,256]{1,0:T(8,128)(2,1)S(1)} %copy-done, bf16[256,2048]{1,0:T(8,128)(2,1)} %param.7), kind=kOutput, calls=%fused_computation.5 | convolution fusion | flops 4294967296 | bytes 36700160 | tf_op jit(solution)/shard_map/dot_general | solution.py:18
  23.2 0.0 copy-start.1
  23.2 27.5 %all-gather.5.cloned.1.call-done = bf16[1024,2048]{1,0:T(8,128)(2,1)} async-done(((bf16[64,2048]{1,0:T(8,128)(2,1)}), bf16[1024,2048]{1,0:T(8,128)(2,1)}) %all-gather.5.cloned.1.call-update) | async-done | bytes 4194320 | tf_op jit(solution)/shard_map/all_gather | solution.py:17
  50.8 54.0 %all-gather.3.cloned.1.call-done = bf16[4096,1024]{0,1:T(8,128)(2,1)} async-done(((bf16[4096,64]{0,1:T(8,128)(2,1)}), bf16[4096,1024]{0,1:T(8,128)(2,1)}) %all-gather.3.cloned.1.call-update) | async-done | bytes 8388624 | tf_op jit(solution)/shard_map/all_gather | solution.py:16
  104.7 25.2 %bitcast_reduce_fusion = f32[8,2048]{1,0:T(8,128)} fusion(f32[4096,2048]{1,0:T(8,128)} %fusion.1, bf16[4096,1024]{0,1:T(8,128)(2,1)} %all-gather.3.cloned.1.call-done, bf16[1024,2048]{1,0:T(8,128)(2,1)} %all-gather.5.cloned.1.call-done), kind=kOutput, calls=%fused_computation | convolution fusion | flops 17196630016 | bytes 46202880 | tf_op jit(solution)/shard_map/dot_general | solution.py:19
  129.9 0.0 reduce-scatter.2.cloned.1.call-update
  129.9 57.1 %reduce-scatter.2.cloned.1.call-done = f32[8,128]{1,0:T(8,128)} async-done(((f32[8,2048]{1,0:T(8,128)}), f32[8,128]{1,0:T(8,128)}) %reduce-scatter.2.cloned.1.call-update) | async-done | bytes 4112 | tf_op jit(solution)/shard_map/reduce_scatter | solution.py:21
  187.0 0.7 broadcast_multiply_fusion
  187.7 0.0 copy-start.2
  187.7 27.8 %all_gather.14 = f32[64,128]{1,0:T(8,128)S(1)} all-gather(f32[8,128]{1,0:T(8,128)S(1)} %broadcast_multiply_fusion), channel_id=1, replica_groups=mesh['dp'=8,'tensor'=16] {'dp'}, dimensions={0}, use_global_device_ids=true | all-gather | bytes 36864 | tf_op jit(solution)/shard_map/all_gather | solution.py:22
  215.5 27.9 %all_gather.15 = f32[64,2048]{1,0:T(8,128)S(1)} all-gather(f32[64,128]{1,0:T(8,128)S(1)} %all_gather.14), channel_id=1, replica_groups=mesh['dp'=8,'tensor'=16] {'tensor'}, dimensions={1}, use_global_device_ids=true | all-gather | bytes 557056 | tf_op jit(solution)/shard_map/all_gather | solution.py:23
  243.5 0.0 copy-done.1
  243.5 2.0 fusion
  245.5 0.0 copy-done.2
Async XLA Ops:
  7.2 1.6 copy-start
  7.2 43.6 %all-gather.5.cloned.1.call-start = ((), (), s32[]{:S(2)}) async-start(), calls=%async_computation.2 | async-start | bytes 4456448 | tf_op jit(solution)/shard_map/all_gather | solution.py:17
  7.9 96.8 %all-gather.3.cloned.1.call-start = ((), (), s32[]{:S(2)}) async-start(), calls=%async_computation.1 | async-start | bytes 8912896 | tf_op jit(solution)/shard_map/all_gather | solution.py:16
  8.7 178.3 %reduce-scatter.2.cloned.1.call-start = ((), (), s32[]{:S(2)}) async-start(), calls=%async_computation.3 | async-start | bytes 69632 | tf_op jit(solution)/shard_map/reduce_scatter | solution.py:21
  23.2 220.2 %copy-start.1 = (f32[128,2048]{1,0:T(8,128)S(1)}, f32[128,2048]{1,0:T(8,128)}, u32[]{:S(2)}) copy-start(f32[128,2048]{1,0:T(8,128)} %param.9) | copy-start | bytes 3145732
  187.7 57.8 %copy-start.2 = (f32[8,128]{1,0:T(8,128)}, f32[8,128]{1,0:T(8,128)S(1)}, u32[]{:S(2)}) copy-start(f32[8,128]{1,0:T(8,128)S(1)} %broadcast_multiply_fusion) | copy-start | bytes 12292
Sparse Core Ops, SparseCore 0:
  9.7 41.0 all-gather.4
  52.5 52.2 all-gather.2
  130.1 56.8 reduce-scatter.1

commit v2 on v1

v2 whole, which is shorter than its diff:
```python
import functools
import math

import jax
import jax.numpy as jnp
from jax import lax
from jax.experimental import pallas as pl
from jax.experimental.pallas import tpu as pltpu
from jax.sharding import PartitionSpec as P

SEQ = 512
NI = 4
NJ = 4
F32 = jnp.float32
BF16 = jnp.bfloat16


def kernel(
    og, inp, op, ip, prev, feat_out, gram_out,
    X, Y, Wo, Wi, own_in, par_in, pz, part, r1buf, fall, lsem, ssem, rsem,
):
    dp = lax.axis_index("dp")
    t = lax.axis_index("tensor")
    x, zh = dp // 2, dp % 2
    y, zl, c = t // 4, (t // 2) % 2, t % 2
    tok = og.shape[0] // 4
    width = op.shape[1]
    ti, wj = tok // NI, width // NJ

    def dev(x_, zh_, y_, zl_, c_):
        return (x_ * 2 + zh_, (y_ * 2 + zl_) * 2 + c_)

    partner = dev(x, zh, y, zl, 1 - c)
    zlo = dev(x, zh, y, 1 - zl, c)
    zlo_other = dev(x, zh, y, 1 - zl, 1 - c)
    zhi = dev(x, 1 - zh, y, 1 - zl, c)
    ypeer = [dev(x, zh, (y + d) % 4, zl, c) for d in (1, 3, 2)]
    xpeer = [dev((x + d) % 4, zh, y, zl, c) for d in (1, 3, 2)]
    tpeer = [(dp, (t + d) % 16) for d in range(1, 16)]
    dpeer = [((dp + d) % 8, t) for d in range(1, 8)]

    copies = []

    def send(src, dst, device):
        k = len(copies)
        cp = pltpu.make_async_remote_copy(
            src_ref=src, dst_ref=dst, send_sem=ssem.at[k], recv_sem=rsem.at[k],
            device_id=device, device_id_type=pl.DeviceIdType.MESH,
        )
        cp.start()
        copies.append(cp)
        return cp

    locals_ = []

    def local(src, dst):
        cp = pltpu.make_async_copy(src, dst, lsem.at[len(locals_)])
        cp.start()
        locals_.append(cp)
        return cp

    blk = zl * 2 + c
    oblk = (1 - zl) * 2 + c

    def rows(b, i=0, n=tok):
        return pl.ds(pl.multiple_of(b * tok + i * n, 256), n)

    def xcol(b):
        return pl.ds(pl.multiple_of(b * 256, 256), 256)

    def ycol(p):
        return pl.ds(pl.multiple_of(p * 128, 128), 128)

    l_in = [local(inp.at[rows(k * 2 + c)], own_in.at[k]) for k in range(2)]
    l_wi = local(ip.at[x], Wi.at[y, zl, c, x])
    l_x = local(og.at[rows(blk)], X.at[:, xcol(blk)])
    l_wo = local(op, Wo.at[xcol(blk)])
    part[...] = jnp.zeros_like(part)

    bar = pltpu.get_barrier_semaphore()
    peers = tpeer + dpeer + [zhi]
    for d in peers:
        pl.semaphore_signal(bar, inc=1, device_id=d, device_id_type=pl.DeviceIdType.MESH)
    pl.semaphore_wait(bar, len(peers))

    s_in = [send(inp.at[rows(k * 2 + 1 - c)], par_in.at[k], partner) for k in range(2)]
    w1 = [send(ip.at[x], Wi.at[y, zl, c, x], d) for d in ypeer]

    def send_x(i):
        r = pl.ds(i * ti, ti)
        return [
            send(og.at[rows((1 - zl) * 2 + c, i, ti)], X.at[r, xcol(blk)], zlo),
            send(og.at[rows((1 - zl) * 2 + 1 - c, i, ti)], X.at[r, xcol(blk)], zlo_other),
        ]

    def send_wo(j):
        cs = pl.ds(j * wj, wj)
        return send(op.at[:, cs], Wo.at[xcol(blk), cs], zhi)

    xs = [send_x(0)]
    wos = [send_wo(0)]
    s_x = send(og.at[rows(zl * 2 + 1 - c)], X.at[:, xcol(blk)], partner)
    s_wo = send(op, Wo.at[xcol(blk)], partner)

    def packed(k):
        a, b = own_in[k], par_in[k]
        first = c == 0
        return jnp.concatenate([jnp.where(first, a, b), jnp.where(first, b, a)], axis=1)

    p_own = y * 2 + zl
    p_oth = y * 2 + 1 - zl
    for k in range(2):
        l_in[k].wait()
        s_in[k].wait_recv()
    pz[...] = packed(1 - zl)
    pzs = []
    for i in range(NI):
        r = pl.ds(i * ti, ti)
        pzs.append(send(pz.at[r], Y.at[r, ycol(p_own)], zlo))
    Y[:, ycol(p_own)] = packed(zl)
    yown = []
    for i in range(NI):
        r = pl.ds(i * ti, ti)
        yown.append([send(Y.at[r, ycol(p_own)], Y.at[r, ycol(p_own)], d) for d in ypeer])
    for i in range(1, NI):
        xs.append(send_x(i))

    l_wi.wait()
    for cp in w1:
        cp.wait_recv()
    w2 = send(Wi.at[:, zl, c, x], Wi.at[:, zl, c, x], zhi)
    for j in range(1, NJ):
        wos.append(send_wo(j))

    def send_w3(cls, j):
        cs = pl.ds(j * wj, wj)
        ref = Wi.at[:, cls, c, x, :, cs]
        return [send(ref, ref, d) for d in xpeer]

    w3a = [send_w3(zl, j) for j in range(NJ)]
    yrel = []
    for i in range(NI):
        r = pl.ds(i * ti, ti)
        pzs[i].wait_recv()
        yrel.append([send(Y.at[r, ycol(p_oth)], Y.at[r, ycol(p_oth)], d) for d in ypeer])
    w2.wait_recv()
    w3b = [send_w3(1 - zl, j) for j in range(NJ)]

    l_x.wait()
    l_wo.wait()
    s_x.wait_recv()
    s_wo.wait_recv()

    def forward(j):
        cs = pl.ds(j * wj, wj)
        wos[j].wait_recv()
        ref = Wo.at[xcol(oblk), cs]
        out = [send(ref, ref, partner)]
        for cp in w3a[j] + w3b[j]:
            cp.wait_recv()
        for zz in range(2):
            ref = Wi.at[:, zz, c, :, :, cs]
            out.append(send(ref, ref, partner))
        return out

    def block(i, j):
        r = pl.ds(pl.multiple_of(i * ti, ti), ti)
        cs = pl.ds(pl.multiple_of(j * wj, wj), wj)
        o = jnp.dot(X[r, :], Wo[:, cs], preferred_element_type=F32)
        wi = Wi[:, :, :, :, :, cs].reshape(Wo.shape[0], wj)
        n = jnp.dot(Y[r, :], wi, preferred_element_type=F32)
        s = jnp.sum(o * n, axis=0, keepdims=True)
        row = pl.ds(blk * 2 + (i * ti) // SEQ, 1)
        part[row, cs] = part[row, cs] + s

    def arrived(i):
        for cp in xs[i] + yown[i] + yrel[i]:
            cp.wait_recv()

    def compute(m):
        lax.fori_loop(0, m + 1, lambda j, u: (block(m, j), u)[1], 0)
        if m:
            lax.fori_loop(0, m, lambda i, u: (block(i, m), u)[1], 0)

    for m in range(NJ):
        fw = forward(m)
        if m:
            compute(m - 1)
        arrived(m)
        for cp in fw:
            cp.wait_recv()
    compute(NJ - 1)

    def tcol(k):
        return pl.ds(pl.multiple_of(k * 128, 128), 128)

    n_before = len(copies)
    r1 = [
        send(part.at[:, tcol((t + d) % 16)], r1buf.at[d], (dp, (t + d) % 16)) for d in range(1, 16)
    ]
    for cp in copies[:n_before]:
        cp.wait_send()
    total = part[:, tcol(t)]
    for cp in r1:
        cp.wait_recv()
    for d in range(1, 16):
        total = total + r1buf[d]
    own = total * F32(1.0 / math.sqrt(SEQ))
    feat_out[...] = own
    drow = pl.ds(pl.multiple_of(dp * 8, 8), 8)
    fall[drow, tcol(t)] = own
    r2 = [send(fall.at[drow, tcol(t)], fall.at[drow, tcol(t)], d) for d in dpeer]
    for cp in r2:
        cp.wait_recv()
    mine = fall.at[:, tcol(t)]
    r3 = [send(mine, mine, dev(x, zh, (y + d // 2) % 4, (zl + d % 2) % 2, c)) for d in range(1, 8)]
    r3p = send(mine, mine, partner)
    r4 = []
    for d in range(1, 8):
        r3[d - 1].wait_recv()
        ref = fall.at[:, tcol(((y - d // 2 + 4) % 4 * 2 + (zl + d % 2) % 2) * 2 + c)]
        r4.append(send(ref, ref, partner))
    r3p.wait_recv()
    for cp in r4:
        cp.wait_recv()
    f = fall[...]
    a = fall[:, tcol(t)]

    def halves(v):
        hi = v.astype(BF16)
        return hi, (v - hi.astype(F32)).astype(BF16)

    fh, fl = halves(f)
    ah, al = halves(a)
    g = lax.dot_general(
        jnp.concatenate([ah, ah, al], axis=0),
        jnp.concatenate([fh, fl, fh], axis=0),
        (((0,), (0,)), ((), ())),
        preferred_element_type=F32,
    )
    gram_out[...] = prev[...] + g * F32(1.0 / 64)
    for cp in copies[n_before:]:
        cp.wait_send()


def local(out_grads, inputs, out_proj, in_proj, prev_gram):
    tok = out_grads.shape[0] // 4
    width = out_proj.shape[1]
    return pl.pallas_call(
        kernel,
        out_shape=(
            jax.ShapeDtypeStruct((8, 128), F32),
            jax.ShapeDtypeStruct((128, width), F32),
        ),
        in_specs=[pl.BlockSpec(memory_space=pl.ANY)] * 4 + [pl.BlockSpec(memory_space=pltpu.VMEM)],
        out_specs=[pl.BlockSpec(memory_space=pltpu.VMEM)] * 2,
        scratch_shapes=[
            pltpu.VMEM((tok, 1024), BF16),
            pltpu.VMEM((tok, 1024), BF16),
            pltpu.VMEM((1024, width), BF16),
            pltpu.VMEM((4, 2, 2, 4, 16, width), BF16),
            pltpu.VMEM((2, tok, 64), BF16),
            pltpu.VMEM((2, tok, 64), BF16),
            pltpu.VMEM((tok, 128), BF16),
            pltpu.VMEM((8, width), F32),
            pltpu.VMEM((16, 8, 128), F32),
            pltpu.VMEM((64, width), F32),
            pltpu.SemaphoreType.DMA((8,)),
            pltpu.SemaphoreType.DMA((140,)),
            pltpu.SemaphoreType.DMA((140,)),
        ],
        compiler_params=pltpu.CompilerParams(
            collective_id=0, has_side_effects=True, vmem_limit_bytes=48 * 2**20
        ),
        name="features_gram",
    )(out_grads, inputs, out_proj, in_proj.reshape(4, 16, width), prev_gram)


def solution(mesh):
    return jax.shard_map(
        local,
        mesh=mesh,
        in_specs=(
            P("dp", "tensor"),
            P("dp", "tensor"),
            P("tensor", None),
            P("tensor", None),
            P("tensor", None),
        ),
        out_specs=(P("dp", "tensor"), P("tensor", None)),
        check_vma=False,
    )
```

time: 252 us -> 71.3 us (0.28)
  waiting for transfers between devices: 140 us -> 0 us
  Pallas kernels: 0 us -> 65.1 us
  blocking collectives: 55.8 us -> 0 us
  matrix products: 41.7 us -> 0 us
  between operations: 13.8 us -> 0.67 us
  local copies, waits for them, and re-layouts: 0.07 us -> 5.34 us
    all_gather x2 -> x0, waiting for transfers between devices: 81.5 us -> none  [the longest x1 54 us: local(): all_inputs = lax.all_gather(inputs, 'tensor', axis=1, tiled=True)]
    pallas_call x0 -> x1, Pallas kernels: none -> 65.1 us  [local(): pl.pallas_call(kernel, out_shape=(jax.ShapeDtypeStruct((8, 128), F32), ja...]
    reduce_scatter x1 -> x0, waiting for transfers between devices: 57.1 us -> none  [local(): lax.psum_scatter(partial_features, 'tensor', scatter_dimension=1, tiled=T...]
    all_gather x2 -> x0, blocking collectives: 55.8 us -> none  [the longest x1 27.9 us: local(): features = lax.all_gather(own_columns, 'tensor', axis=1, tiled=True)]
    dot_general x3 -> x0, matrix products: 41.7 us -> none  [the longest x1 25.2 us: local(): jnp.dot(all_inputs, all_in_proj, preferred_element_type=jnp.float32)]
    unnamed x6 -> x9, local copies, waits for them, and re-layouts: 0.07 us -> 5.34 us
  transfers between devices with their start and end apart: 3 -> 0, of which waited for: 3 -> 0; matrix products, arithmetic and copies ran while one was open for 6% -> 0% of each run, Pallas kernels for 0% -> 0%
where the time goes in v2:
time: 71.3 us; the launch traced here: 71.1 us
  Pallas kernels  65.1 us (91%)
  local copies, waits for them, and re-layouts  5.34 us (7%)
    pallas_call x1, Pallas kernels, local(): pl.pallas_call(kernel, out_shape=(jax.ShapeDtypeStruct((8, 128), F32), ja...  65.1 us
    unnamed x9, local copies, waits for them, and re-layouts  5.34 us

profile of v2, /device:TPU:1, one launch (start us, length us, event | category | flops | bytes accessed | tf_op | source)
XLA Modules:
  0.0 71.1 jit_solution(8790722494652492145)
XLA Ops:
  0.6 0.0 copy-start
  0.6 1.6 %copy.7.inp = bf16[4096,64]{1,0:T(8,128)(2,1)S(1)} copy(bf16[4096,64]{0,1:T(8,128)(2,1)} %param.6) | data formatting | bytes 1048576 | tf_op args[1]
  2.2 0.0 copy-done
  2.3 0.0 copy-start.1
  2.3 1.2 %copy-done.1 = f32[128,2048]{1,0:T(8,128)S(1)} copy-done((f32[128,2048]{1,0:T(8,128)S(1)}, f32[128,2048]{1,0:T(8,128)}, u32[]{:S(2)}) %copy-start.1) | copy-done | bytes 1048600
  3.5 0.0 copy-start.2
  3.5 0.9 %copy-done.2 = bf16[64,2048]{1,0:T(8,128)(2,1)S(1)} copy-done((bf16[64,2048]{1,0:T(8,128)(2,1)S(1)}, bf16[64,2048]{1,0:T(8,128)(2,1)}, u32[]{:S(2)}) %copy-start.2) | copy-done | bytes 262168
  4.4 65.1 %features_gram.1 = (f32[8,128]{1,0:T(8,128)S(1)}, f32[128,2048]{1,0:T(8,128)S(1)}) custom-call(bf16[4096,256]{1,0:T(8,128)(2,1)} %og.1, bf16[4096,64]{1,0:T(8,128)(2,1)S(1)} %copy.7.inp, bf16[256,2048]{1,0:T(8,128)(2,1)S(1)} %copy-done, bf16[4,16,2048]{2,1,0:T(8,128)(2,1)S(1)} %bitcast.1, f32[128,2048]{1,0:T(8,128)S(1)} %copy-done.1), custom_call_target="tpu_custom_call" | custom-call | tf_op jit(solution)/shard_map/features_gram/pallas_call | solution.py:249
  69.5 0.6 copy.10
  70.1 1.0 %copy.11 = f32[128,2048]{1,0:T(8,128)} copy(f32[128,2048]{1,0:T(8,128)S(1)} %get-tuple-element.5) | data formatting | bytes 2097152
Async XLA Ops:
  0.6 1.6 %copy-start = (bf16[256,2048]{1,0:T(8,128)(2,1)S(1)}, bf16[256,2048]{1,0:T(8,128)(2,1)}, u32[]{:S(2)}) copy-start(bf16[256,2048]{1,0:T(8,128)(2,1)} %op.1) | copy-start | bytes 3145732
  2.3 1.2 %copy-start.1 = (f32[128,2048]{1,0:T(8,128)S(1)}, f32[128,2048]{1,0:T(8,128)}, u32[]{:S(2)}) copy-start(f32[128,2048]{1,0:T(8,128)} %prev.1) | copy-start | bytes 3145732
  3.5 0.9 %copy-start.2 = (bf16[64,2048]{1,0:T(8,128)(2,1)S(1)}, bf16[64,2048]{1,0:T(8,128)(2,1)}, u32[]{:S(2)}) copy-start(bf16[64,2048]{1,0:T(8,128)(2,1)} %param.8) | copy-start | bytes 786436

commit v3 on v1

v3 whole, which is shorter than its diff:
```python
import math

import jax
import jax.numpy as jnp
from jax import lax
from jax.experimental import pallas as pl
from jax.experimental.pallas import tpu as pltpu
from jax.sharding import PartitionSpec as P

SEQ = 512
NI = 4
NJ = 4
F32 = jnp.float32
BF16 = jnp.bfloat16
MESH = pl.DeviceIdType.MESH


class Copy:
    def __init__(self, cp, remote):
        self.cp, self.remote, self.sent, self.got = cp, remote, not remote, False
        cp.start()

    def wait_recv(self):
        if self.got:
            return
        if self.remote:
            self.cp.wait_recv()
        else:
            self.cp.wait()
        self.got = True

    def wait_send(self):
        if not self.sent:
            self.cp.wait_send()
        self.sent = True


def kernel(
    og, inp, op, ip, prev, feat_out, gram_out, fall, X, Y, Wo, Wi, pk, pz, part, rbuf, lsem, ssem, rsem
):
    dp = lax.axis_index("dp")
    t = lax.axis_index("tensor")
    x, zh = dp // 2, dp % 2
    y, zl, c = t // 4, (t // 2) % 2, t % 2
    tok = og.shape[0] // 4
    width = op.shape[1]
    ti, wj = tok // NI, width // NJ

    def dev(x_, zh_, y_, zl_, c_):
        return (x_ * 2 + zh_, (y_ * 2 + zl_) * 2 + c_)

    partner = dev(x, zh, y, zl, 1 - c)
    zlo = dev(x, zh, y, 1 - zl, c)
    zlo_other = dev(x, zh, y, 1 - zl, 1 - c)
    zhi = dev(x, 1 - zh, y, 1 - zl, c)
    order = (1, 3, 2)
    zl_own, zl_oth = 0, 1
    ypeer = [dev(x, zh, (y + d) % 4, zl, c) for d in order]
    xdir = (1 + 2 * c, 3 - 2 * c)
    xpeer = [dev((x + d) % 4, zh, y, zl, c) for d in xdir]

    def shifted(dx, dz, sign):
        z_ = (zh * 2 + zl + 4 + sign * dz) % 4
        return ((x + 4 + sign * dx) % 4, z_ // 2, z_ % 2)

    steps = [(dx, dz) for dx in range(4) for dz in range(4) if dx or dz]
    steps.sort(key=lambda s: min(s[0], 4 - s[0]) + min(s[1], 4 - s[1]))

    def plane(s):
        x_, zh_, zl_ = shifted(*s, 1)
        return dev(x_, zh_, y, zl_, c)

    copies, locals_ = [], []

    def send(src, dst, device):
        k = len(copies)
        copies.append(
            Copy(
                pltpu.make_async_remote_copy(
                    src_ref=src, dst_ref=dst, send_sem=ssem.at[k], recv_sem=rsem.at[k],
                    device_id=device, device_id_type=MESH,
                ),
                True,
            )
        )
        return copies[-1]

    def local(src, dst):
        locals_.append(Copy(pltpu.make_async_copy(src, dst, lsem.at[len(locals_)]), False))
        return locals_[-1]

    blk = zl * 2 + c
    d_near, d_far = xdir[1], xdir[0]
    oblk = (1 - zl) * 2 + c
    p_own = y * 2 + zl
    p_oth = y * 2 + 1 - zl

    def rows(b, start=0, size=tok):
        return pl.ds(pl.multiple_of(b * tok + start, 128), size)

    def wrow(b):
        return pl.ds(pl.multiple_of(b * 256, 256), 256)

    def col(d):
        return (x + d) % 4

    def cols(d):
        return pl.ds(pl.multiple_of(col(d) * wj, wj), wj)

    def irow(core):
        return pl.ds(pl.multiple_of(core * 64, 64), 64)

    l_in = [local(inp.at[:, rows(k * 2 + c)], pk.at[k, irow(c)]) for k in range(2)]
    l_wi = local(ip.at[:, cols(0)], Wi.at[x, y, zl, c])
    part[...] = jnp.zeros_like(part)

    bar = pltpu.get_barrier_semaphore()
    peers = [partner, zlo_other] + ypeer + [plane(s) for s in steps]
    for d in peers:
        pl.semaphore_signal(bar, inc=1, device_id=d, device_id_type=MESH)
    pl.semaphore_wait(bar, len(peers))

    s_in = [
        send(inp.at[:, rows(k * 2 + 1 - c)], pk.at[k, irow(c)], partner) for k in (0, 1)
    ]
    w_own = ip.at[:, cols(0)]
    w_to = Wi.at[x, y, zl, c]
    w1 = [send(w_own, w_to, d) for d in ypeer]
    w2 = [send(w_own, w_to, zhi)]
    w3 = {}
    w3[zl_own, 0] = [send(w_own, w_to, d) for d in xpeer]

    def send_wo(d, start, size):
        r = pl.ds(start, size)
        to = pl.ds(pl.multiple_of(blk * 256 + start, 128), size)
        return send(op.at[r, cols(d)], Wo.at[col(d), to], zhi)

    def send_x(start, size):
        r = pl.ds(start, size)
        return [
            send(og.at[rows((1 - zl) * 2 + c, start, size)], X.at[blk, r], zlo),
            send(og.at[rows((1 - zl) * 2 + 1 - c, start, size)], X.at[blk, r], zlo_other),
        ]

    xs = [send_x(0, ti // 2)]
    wo_x = [send_wo(0, 0, 128)]

    for k in range(2):
        l_in[k].wait_recv()
        s_in[k].wait_recv()
    pzs = []
    for i in range(NI):
        r = pl.ds(i * ti, ti)
        pz[r, :] = pk[1 - zl, :, r].T
        pzs.append(send(pz.at[r], Y.at[p_own, r], zlo))
    xs[0] += send_x(ti // 2, ti // 2)
    for i in range(1, NI):
        xs.append(send_x(i * ti, ti))
    yown, yrel, yfar, d_wi = [], [], {}, {}

    def send_own(i):
        r = pl.ds(i * ti, ti)
        Y[p_own, r, :] = pk[zl, :, r].T
        yown.append([send(Y.at[p_own, r], Y.at[p_own, r], d) for d in ypeer[:2]])

    def pass_w1(k):
        w1[k].wait_recv()
        ref = Wi.at[x, (y + 4 - order[k]) % 4, zl, c]
        w2.append(send(ref, ref, zhi))
        w3[zl_own, k + 1] = [send(ref, ref, d) for d in xpeer]

    def pass_w2(k):
        w2[k].wait_recv()
        y_ = y if k == 0 else (y + 4 - order[k - 1]) % 4
        ref = Wi.at[x, y_, 1 - zl, c]
        w3[zl_oth, k] = [send(ref, ref, d) for d in xpeer]

    def relay(i):
        r = pl.ds(i * ti, ti)
        pzs[i].wait_recv()
        yrel.append([send(Y.at[p_oth, r], Y.at[p_oth, r], d) for d in ypeer[:2]])

    def pass_y(cps, cls, i):
        k, up = i % 2, (1, 3)[i % 2]
        cps[i][k].wait_recv()
        ref = Y.at[(y + 4 - up) % 4 * 2 + cls, pl.ds(i * ti, ti)]
        return send(ref, ref, ypeer[k])

    def own_far(i):
        yfar[0, i] = pass_y(yown, zl, i)

    def rel_far(i):
        yfar[1, i] = pass_y(yrel, 1 - zl, i)

    send_own(0)
    send_own(1)
    pass_w1(0)
    pass_w1(1)
    pass_w2(0)
    pass_w1(2)
    wo_x.append(send_wo(0, 128, 128))
    wo_2 = send_wo(2, 0, 256)
    wo_far = send_wo(d_far, 0, 256)
    s_wo = [send(op.at[:, cols(d)], Wo.at[col(d), wrow(blk)], partner) for d in range(NJ)]
    s_x = send(og.at[rows(zl * 2 + 1 - c)], X.at[blk], partner)
    l_x = local(og.at[rows(blk)], X.at[blk])
    l_wo = [local(op.at[:, cols(d)], Wo.at[col(d), wrow(blk)]) for d in range(NJ)]
    l_prev = local(prev, gram_out)
    relay(0)
    own_far(0)
    relay(1)
    pass_w2(1)
    own_far(1)
    pass_w2(2)
    rel_far(0)
    pass_w2(3)
    l_wi.wait_recv()
    ref = Wi.at[x, :, :, c]
    d_wi[0] = send(ref, ref, partner)
    rel_far(1)

    def pass_x(cls, k):
        for q in range(4):
            w3[cls, q][k].wait_recv()
        ref = Wi.at[(x + 4 - xdir[k]) % 4, :, (zl, 1 - zl)[cls], c]
        return send(ref, ref, xpeer[k])

    x_a = pass_x(zl_own, 1)
    send_own(2)
    send_own(3)
    relay(2)
    relay(3)
    for cp in wo_x:
        cp.wait_recv()
    ref = Wo.at[x, wrow(oblk)]
    d_wo = [send(ref, ref, partner)]
    x_b = pass_x(zl_oth, 0)
    wo_near = send(ref, ref, xpeer[0])

    def block(start, size, js):
        r = pl.ds(start, size)
        xv = jnp.concatenate([X[b, r, :] for b in range(4)], axis=1)
        yv = jnp.concatenate([Y[p, r, :] for p in range(8)], axis=1)
        wo = jnp.concatenate([Wo[j] for j in js], axis=1)
        wi = jnp.concatenate([Wi[j].reshape(Wo.shape[1], wj) for j in js], axis=1)
        o = jnp.dot(xv, wo, preferred_element_type=F32)
        n = jnp.dot(yv, wi, preferred_element_type=F32)
        s = jnp.sum(o * n, axis=0, keepdims=True)
        clip = start // SEQ
        for q, j in enumerate(js):
            for k in range(4):
                row = pl.ds(j * 4 + k, 1)
                at = q * wj + k * 128
                part[clip, row, :] = part[clip, row, :] + s[:, at : at + 128]

    def arrived(i):
        for cp in xs[i] + yown[i] + yrel[i] + [yfar[0, i], yfar[1, i]]:
            cp.wait_recv()

    def compute(start, size, first, step, count):
        def body(m, u):
            block(start, size, [(x + first + step * m) % 4])
            return u

        lax.fori_loop(0, count, body, 0)

    def compute_all(start, size):
        def body(m, u):
            block(start, size, [(x + 2 * m) % 4, (x + 2 * m + 1) % 4])
            return u

        lax.fori_loop(0, 2, body, 0)

    l_x.wait_recv()
    for cp in l_wo + [s_x] + s_wo:
        cp.wait_recv()
    arrived(0)
    d_wi[0].wait_recv()
    d_wo[0].wait_recv()
    compute(0, ti, 0, 1, 1)
    for q in range(4):
        for k in range(2):
            w3[zl_own, q][k].wait_recv()
            w3[zl_oth, q][k].wait_recv()
    for d in (1, 3):
        ref = Wi.at[col(d), :, :, c]
        d_wi[d] = send(ref, ref, partner)
    own_far(2)
    own_far(3)
    arrived(1)
    compute(ti, ti, 0, 1, 1)
    rel_far(2)
    rel_far(3)
    x_a.wait_recv()
    x_b.wait_recv()
    ref = Wi.at[col(2), :, :, c]
    d_wi[2] = send(ref, ref, partner)
    wo_2.wait_recv()
    ref = Wo.at[col(2), wrow(oblk)]
    d_wo.append(send(ref, ref, partner))
    d_wi[2].wait_recv()
    d_wo[1].wait_recv()
    compute(0, 2 * ti, 2, 1, 1)
    for cp, d in ((wo_far, d_far), (wo_near, d_near)):
        cp.wait_recv()
        ref = Wo.at[col(d), wrow(oblk)]
        d_wo.append(send(ref, ref, partner))
    arrived(2)
    compute(2 * ti, ti, 0, 2, 2)
    for k in range(2):
        d_wi[2 * k + 1].wait_recv()
        d_wo[2 + k].wait_recv()
    me = dp * 2 + zl

    def add_up(clip):
        return [
            send(part.at[clip], rbuf.at[clip, d - 1], dev(x, zh, (y + d) % 4, zl, c))
            for d in range(1, 4)
        ]

    def spread(clip, cps):
        for cp in cps:
            cp.wait_recv()
        own = (part[clip] + rbuf[clip, 0]) + (rbuf[clip, 1] + rbuf[clip, 2])
        fall[clip, me, c] = own * F32(1.0 / math.sqrt(SEQ))
        mine = fall.at[clip, me, c]
        return [send(mine, mine, plane(s)) for s in steps], [send(mine, mine, partner)]

    def hand_over(clip, cps, out):
        for s, cp in zip(steps, cps):
            cp.wait_recv()
            x_, zh_, zl_ = shifted(*s, -1)
            ref = fall.at[clip, (x_ * 2 + zh_) * 2 + zl_, c]
            out.append(send(ref, ref, partner))

    compute(0, 2 * ti, 1, 2, 2)
    main = list(copies)
    r1 = add_up(0)
    compute(2 * ti, ti, 1, 2, 2)
    r2, r3 = spread(0, r1)
    for cp in main:
        cp.wait_send()
    l_prev.wait_recv()
    arrived(3)
    compute_all(3 * ti, ti)
    r1b = add_up(1)
    hand_over(0, r2, r3)
    r2b, r3b = spread(1, r1b)
    for cp in copies:
        if not cp.sent and cp not in r2b and cp not in r3b:
            cp.wait_send()
    hand_over(1, r2b, r3b)
    for cp in r3 + r3b:
        cp.wait_recv()

    flat = fall.reshape(2 * 16 * 2 * 16, 128)

    def clips(j, lane):
        return flat[pl.ds(j * 4 + lane, 64, stride=16), :]

    def halves(v):
        hi = v.astype(BF16)
        return hi, (v - hi.astype(F32)).astype(BF16)

    ah, al = halves(clips(y, t % 4))
    a3 = jnp.concatenate([ah, ah, al], axis=0)
    for j in range(NJ):
        fh, fl = halves(jnp.concatenate([clips(j, lane) for lane in range(4)], axis=1))
        g = lax.dot_general(
            a3,
            jnp.concatenate([fh, fl, fh], axis=0),
            (((0,), (0,)), ((), ())),
            preferred_element_type=F32,
        )
        cs = pl.ds(j * wj, wj)
        gram_out[:, cs] = gram_out[:, cs] + g * F32(1.0 / 64)
    for k in range(8):
        row = ((k % 2 * 16 + dp * 2 + k // 4) * 2 + k // 2 % 2) * 16 + y * 4 + t % 4
        feat_out[k : k + 1, :] = flat[pl.ds(row, 1), :]
    for cp in copies:
        if not cp.sent:
            cp.wait_send()


def local(out_grads, inputs, out_proj, in_proj, prev_gram):
    tok = out_grads.shape[0] // 4
    width = out_proj.shape[1]
    wj = width // NJ
    vmem = pl.BlockSpec(memory_space=pltpu.VMEM)
    hbm = pl.BlockSpec(memory_space=pltpu.HBM)
    operands = (out_grads, inputs.T, out_proj, in_proj, prev_gram)
    return pl.pallas_call(
        kernel,
        out_shape=(
            jax.ShapeDtypeStruct((8, 128), F32),
            jax.ShapeDtypeStruct((128, width), F32),
        ),
        in_specs=[hbm] * 5,
        out_specs=[vmem] * 2,
        scratch_shapes=[
            pltpu.VMEM((2, 16, 2, 16, 128), F32),
            pltpu.VMEM((4, tok, 256), BF16),
            pltpu.VMEM((8, tok, 128), BF16),
            pltpu.VMEM((NJ, 1024, wj), BF16),
            pltpu.VMEM((NJ, 4, 2, 2, 64, wj), BF16),
            pltpu.VMEM((2, 128, tok), BF16),
            pltpu.VMEM((tok, 128), BF16),
            pltpu.VMEM((2, 16, 128), F32),
            pltpu.VMEM((2, 3, 16, 128), F32),
            pltpu.SemaphoreType.DMA((10,)),
            pltpu.SemaphoreType.DMA((160,)),
            pltpu.SemaphoreType.DMA((160,)),
        ],
        compiler_params=pltpu.CompilerParams(
            collective_id=0, has_side_effects=True, vmem_limit_bytes=40 * 2**20
        ),
        name="features_gram",
    )(*[pltpu.with_memory_space_constraint(a, pltpu.HBM) for a in operands])


def solution(mesh):
    return jax.shard_map(
        local,
        mesh=mesh,
        in_specs=(
            P("dp", "tensor"),
            P("dp", "tensor"),
            P("tensor", None),
            P("tensor", None),
            P("tensor", None),
        ),
        out_specs=(P("dp", "tensor"), P("tensor", None)),
        check_vma=False,
    )
```

time: 252 us -> 60.4 us (0.24)
  waiting for transfers between devices: 140 us -> 0 us
  Pallas kernels: 0 us -> 58.1 us
  blocking collectives: 55.8 us -> 0 us
  matrix products: 41.7 us -> 0 us
  between operations: 13.8 us -> 0.64 us
    all_gather x2 -> x0, waiting for transfers between devices: 81.5 us -> none  [the longest x1 54 us: local(): all_inputs = lax.all_gather(inputs, 'tensor', axis=1, tiled=True)]
    pallas_call x0 -> x1, Pallas kernels: none -> 58.1 us  [local(): pl.pallas_call(kernel, out_shape=(jax.ShapeDtypeStruct((8, 128), F32), ja...]
    reduce_scatter x1 -> x0, waiting for transfers between devices: 57.1 us -> none  [local(): lax.psum_scatter(partial_features, 'tensor', scatter_dimension=1, tiled=T...]
    all_gather x2 -> x0, blocking collectives: 55.8 us -> none  [the longest x1 27.9 us: local(): features = lax.all_gather(own_columns, 'tensor', axis=1, tiled=True)]
    dot_general x3 -> x0, matrix products: 41.7 us -> none  [the longest x1 25.2 us: local(): jnp.dot(all_inputs, all_in_proj, preferred_element_type=jnp.float32)]
  transfers between devices with their start and end apart: 3 -> 0, of which waited for: 3 -> 0; matrix products, arithmetic and copies ran while one was open for 6% -> 0% of each run, Pallas kernels for 0% -> 0%
where the time goes in v3:
time: 60.4 us; the launch traced here: 60.3 us
  Pallas kernels  58.1 us (96%)
  local copies, waits for them, and re-layouts  1.56 us (3%)
  between operations  0.64 us (1%)
    pallas_call x1, Pallas kernels, local(): pl.pallas_call(kernel, out_shape=(jax.ShapeDtypeStruct((8, 128), F32), ja...  58.1 us
    unnamed x2, local copies, waits for them, and re-layouts  1.56 us

profile of v3, /device:TPU:1, one launch (start us, length us, event | category | flops | bytes accessed | tf_op | source)
XLA Modules:
  0.0 60.3 jit_solution(2610619531311387959)
XLA Ops:
  0.6 58.1 %features_gram.1 = (f32[8,128]{1,0:T(8,128)S(1)}, f32[128,2048]{1,0:T(8,128)S(1)}) custom-call(bf16[4096,256]{1,0:T(8,128)(2,1)} %og.1, bf16[64,4096]{1,0:T(8,128)(2,1)} %bitcast.1, bf16[256,2048]{1,0:T(8,128)(2,1)} %op.1, bf16[64,2048]{1,0:T(8,128)(2,1)} %ip.1, f32[128,2048]{1,0:T(8,128)} %prev.1), custom_call_target="tpu_custom_call" | custom-call | tf_op jit(solution)/shard_map/features_gram/pallas_call | solution.py:392
  58.7 0.6 copy.9
  59.3 1.0 %copy.10 = f32[128,2048]{1,0:T(8,128)} copy(f32[128,2048]{1,0:T(8,128)S(1)} %get-tuple-element.5) | data formatting | bytes 2097152

commit v4 on v3

--- a/solution.py
+++ b/solution.py
@@ -36,7 +36,7 @@
 
 
 def kernel(
-    og, inp, op, ip, prev, feat_out, gram_out, fall, X, Y, Wo, Wi, pk, pz, part, rbuf, lsem, ssem, rsem
+    og, inp, op, ip, prev, feat_out, gram_out, fall, X, Y, Wo, Wi, pk, pz, part, rbuf, lsem, ssem, rsem, word
 ):
     dp = lax.axis_index("dp")
     t = lax.axis_index("tensor")
@@ -66,9 +66,9 @@
     steps = [(dx, dz) for dx in range(4) for dz in range(4) if dx or dz]
     steps.sort(key=lambda s: min(s[0], 4 - s[0]) + min(s[1], 4 - s[1]))
 
-    def plane(s):
+    def plane(s, core=c):
         x_, zh_, zl_ = shifted(*s, 1)
-        return dev(x_, zh_, y, zl_, c)
+        return dev(x_, zh_, y, zl_, core)
 
     copies, locals_ = [], []
 
@@ -90,7 +90,8 @@
         return locals_[-1]
 
     blk = zl * 2 + c
-    d_near, d_far = xdir[1], xdir[0]
+    d_near, d_far = 3, 1
+    xsides = [dev((x + d) % 4, zh, y, zl, c) for d in (1, 3)]
     oblk = (1 - zl) * 2 + c
     p_own = y * 2 + zl
     p_oth = y * 2 + 1 - zl
@@ -115,10 +116,20 @@
     part[...] = jnp.zeros_like(part)
 
     bar = pltpu.get_barrier_semaphore()
-    peers = [partner, zlo_other] + ypeer + [plane(s) for s in steps]
+    near = [partner] + [plane(s) for s in steps[:4]]
+    peers = [zlo_other] + ypeer + near
     for d in peers:
         pl.semaphore_signal(bar, inc=1, device_id=d, device_id_type=MESH)
     pl.semaphore_wait(bar, len(peers))
+
+    def pass_word(k):
+        if k:
+            pl.semaphore_wait(word.at[k - 1], len(near))
+        if k < 4:
+            for d in near:
+                pl.semaphore_signal(word.at[k], inc=1, device_id=d, device_id_type=MESH)
+
+    pass_word(0)
 
     s_in = [
         send(inp.at[:, rows(k * 2 + 1 - c)], pk.at[k, irow(c)], partner) for k in (0, 1)
@@ -128,7 +139,7 @@
     w1 = [send(w_own, w_to, d) for d in ypeer]
     w2 = [send(w_own, w_to, zhi)]
     w3 = {}
-    w3[zl_own, 0] = [send(w_own, w_to, d) for d in xpeer]
+    w3[zl_own, 0] = [send(w_own, w_to, d) for d in xsides]
 
     def send_wo(d, start, size):
         r = pl.ds(start, size)
@@ -167,7 +178,7 @@
         w1[k].wait_recv()
         ref = Wi.at[x, (y + 4 - order[k]) % 4, zl, c]
         w2.append(send(ref, ref, zhi))
-        w3[zl_own, k + 1] = [send(ref, ref, d) for d in xpeer]
+        w3[zl_own, k + 1] = [send(ref, ref, d) for d in xsides]
 
     def pass_w2(k):
         w2[k].wait_recv()
@@ -199,8 +210,8 @@
     pass_w2(0)
     pass_w1(2)
     wo_x.append(send_wo(0, 128, 128))
+    wo_far = send_wo(d_far, 0, 256)
     wo_2 = send_wo(2, 0, 256)
-    wo_far = send_wo(d_far, 0, 256)
     s_wo = [send(op.at[:, cols(d)], Wo.at[col(d), wrow(blk)], partner) for d in range(NJ)]
     s_x = send(og.at[rows(zl * 2 + 1 - c)], X.at[blk], partner)
     l_x = local(og.at[rows(blk)], X.at[blk])
@@ -219,23 +230,24 @@
     d_wi[0] = send(ref, ref, partner)
     rel_far(1)
 
-    def pass_x(cls, k):
+    def pass_x(cls, k, d, device):
         for q in range(4):
             w3[cls, q][k].wait_recv()
-        ref = Wi.at[(x + 4 - xdir[k]) % 4, :, (zl, 1 - zl)[cls], c]
-        return send(ref, ref, xpeer[k])
-
-    x_a = pass_x(zl_own, 1)
+        ref = Wi.at[(x + 4 - d) % 4, :, (zl, 1 - zl)[cls], c]
+        return send(ref, ref, device)
+
+    x_a = pass_x(zl_own, 1, 3, xsides[1])
     send_own(2)
     send_own(3)
     relay(2)
     relay(3)
+    pass_word(1)
     for cp in wo_x:
         cp.wait_recv()
     ref = Wo.at[x, wrow(oblk)]
     d_wo = [send(ref, ref, partner)]
-    x_b = pass_x(zl_oth, 0)
-    wo_near = send(ref, ref, xpeer[0])
+    x_b = pass_x(zl_oth, 0, xdir[0], xpeer[0])
+    wo_near = send(ref, ref, xsides[0])
 
     def block(start, size, js):
         r = pl.ds(start, size)
@@ -287,10 +299,18 @@
         d_wi[d] = send(ref, ref, partner)
     own_far(2)
     own_far(3)
+    pass_word(2)
     arrived(1)
     compute(ti, ti, 0, 1, 1)
     rel_far(2)
     rel_far(3)
+    wo_far.wait_recv()
+    ref = Wo.at[col(d_far), wrow(oblk)]
+    d_wo.append(send(ref, ref, partner))
+    for cp in (d_wi[1], d_wi[3], d_wo[1]):
+        cp.wait_recv()
+    pass_word(3)
+    compute(0, 2 * ti, d_far, 1, 1)
     x_a.wait_recv()
     x_b.wait_recv()
     ref = Wi.at[col(2), :, :, c]
@@ -298,18 +318,17 @@
     wo_2.wait_recv()
     ref = Wo.at[col(2), wrow(oblk)]
     d_wo.append(send(ref, ref, partner))
+    arrived(2)
+    compute(2 * ti, ti, 0, d_far, 2)
     d_wi[2].wait_recv()
-    d_wo[1].wait_recv()
+    d_wo[2].wait_recv()
+    pass_word(4)
     compute(0, 2 * ti, 2, 1, 1)
-    for cp, d in ((wo_far, d_far), (wo_near, d_near)):
-        cp.wait_recv()
-        ref = Wo.at[col(d), wrow(oblk)]
-        d_wo.append(send(ref, ref, partner))
-    arrived(2)
-    compute(2 * ti, ti, 0, 2, 2)
-    for k in range(2):
-        d_wi[2 * k + 1].wait_recv()
-        d_wo[2 + k].wait_recv()
+    wo_near.wait_recv()
+    ref = Wo.at[col(d_near), wrow(oblk)]
+    d_wo.append(send(ref, ref, partner))
+    compute(2 * ti, ti, 2, 1, 1)
+    d_wo[3].wait_recv()
     me = dp * 2 + zl
 
     def add_up(clip):
@@ -324,19 +343,23 @@
         own = (part[clip] + rbuf[clip, 0]) + (rbuf[clip, 1] + rbuf[clip, 2])
         fall[clip, me, c] = own * F32(1.0 / math.sqrt(SEQ))
         mine = fall.at[clip, me, c]
-        return [send(mine, mine, plane(s)) for s in steps], [send(mine, mine, partner)]
+        out = [send(mine, mine, plane(s)) for s in steps[::-1]][::-1]
+        both = [send(mine, mine, plane(s, 1 - c)) for s in steps[10:]] if clip else []
+        return out, both + [send(mine, mine, partner)]
 
     def hand_over(clip, cps, out):
-        for s, cp in zip(steps, cps):
+        for k, (s, cp) in enumerate(zip(steps, cps)):
             cp.wait_recv()
+            if clip and k >= 10:
+                continue
             x_, zh_, zl_ = shifted(*s, -1)
             ref = fall.at[clip, (x_ * 2 + zh_) * 2 + zl_, c]
             out.append(send(ref, ref, partner))
 
-    compute(0, 2 * ti, 1, 2, 2)
+    compute(0, 2 * ti, d_near, 1, 1)
     main = list(copies)
     r1 = add_up(0)
-    compute(2 * ti, ti, 1, 2, 2)
+    compute(2 * ti, ti, d_near, 1, 1)
     r2, r3 = spread(0, r1)
     for cp in main:
         cp.wait_send()
@@ -410,6 +433,7 @@
             pltpu.SemaphoreType.DMA((10,)),
             pltpu.SemaphoreType.DMA((160,)),
             pltpu.SemaphoreType.DMA((160,)),
+            pltpu.SemaphoreType.REGULAR((4,)),
         ],
         compiler_params=pltpu.CompilerParams(
             collective_id=0, has_side_effects=True, vmem_limit_bytes=40 * 2**20

time: 60.4 us -> 58.9 us (0.975)
  Pallas kernels: 58.1 us -> 56.6 us
    pallas_call x1, Pallas kernels: 58.1 us -> 56.6 us  [local(): pl.pallas_call(kernel, out_shape=(jax.ShapeDtypeStruct((8, 128), F32), ja...]
where the time goes in v4:
time: 58.9 us; the launch traced here: 58.8 us
  Pallas kernels  56.6 us (96%)
  local copies, waits for them, and re-layouts  1.56 us (3%)
  between operations  0.64 us (1%)
    pallas_call x1, Pallas kernels, local(): pl.pallas_call(kernel, out_shape=(jax.ShapeDtypeStruct((8, 128), F32), ja...  56.6 us
    unnamed x2, local copies, waits for them, and re-layouts  1.56 us

profile of v4, /device:TPU:1, one launch (start us, length us, event | category | flops | bytes accessed | tf_op | source)
XLA Modules:
  0.0 58.8 jit_solution(10692282396624307016)
XLA Ops:
  0.6 56.6 %features_gram.1 = (f32[8,128]{1,0:T(8,128)S(1)}, f32[128,2048]{1,0:T(8,128)S(1)}) custom-call(bf16[4096,256]{1,0:T(8,128)(2,1)} %og.1, bf16[64,4096]{1,0:T(8,128)(2,1)} %bitcast.1, bf16[256,2048]{1,0:T(8,128)(2,1)} %op.1, bf16[64,2048]{1,0:T(8,128)(2,1)} %ip.1, f32[128,2048]{1,0:T(8,128)} %prev.1), custom_call_target="tpu_custom_call" | custom-call | tf_op jit(solution)/shard_map/features_gram/pallas_call | solution.py:415
  57.2 0.6 %copy.9 = f32[8,128]{1,0:T(8,128)} copy(f32[8,128]{1,0:T(8,128)S(1)} %get-tuple-element.4) | data formatting | bytes 8192
  57.8 1.0 %copy.10 = f32[128,2048]{1,0:T(8,128)} copy(f32[128,2048]{1,0:T(8,128)S(1)} %get-tuple-element.5) | data formatting | bytes 2097152

commit v5 on v4

--- a/solution.py
+++ b/solution.py
@@ -111,8 +111,9 @@
     def irow(core):
         return pl.ds(pl.multiple_of(core * 64, 64), 64)
 
+    l_wi = local(ip.at[:, cols(0)], Wi.at[x, y, zl, c])
     l_in = [local(inp.at[:, rows(k * 2 + c)], pk.at[k, irow(c)]) for k in range(2)]
-    l_wi = local(ip.at[:, cols(0)], Wi.at[x, y, zl, c])
+    l_wo = {d: local(op.at[:, cols(d)], Wo.at[col(d), wrow(blk)]) for d in (0, 1, 2, 3)}
     part[...] = jnp.zeros_like(part)
 
     bar = pltpu.get_barrier_semaphore()
@@ -134,17 +135,17 @@
     s_in = [
         send(inp.at[:, rows(k * 2 + 1 - c)], pk.at[k, irow(c)], partner) for k in (0, 1)
     ]
-    w_own = ip.at[:, cols(0)]
-    w_to = Wi.at[x, y, zl, c]
+    l_wi.wait_recv()
+    w_own = w_to = Wi.at[x, y, zl, c]
     w1 = [send(w_own, w_to, d) for d in ypeer]
     w2 = [send(w_own, w_to, zhi)]
     w3 = {}
     w3[zl_own, 0] = [send(w_own, w_to, d) for d in xsides]
 
     def send_wo(d, start, size):
-        r = pl.ds(start, size)
-        to = pl.ds(pl.multiple_of(blk * 256 + start, 128), size)
-        return send(op.at[r, cols(d)], Wo.at[col(d), to], zhi)
+        l_wo[d].wait_recv()
+        ref = Wo.at[col(d), pl.ds(pl.multiple_of(blk * 256 + start, 128), size)]
+        return send(ref, ref, zhi)
 
     def send_x(start, size):
         r = pl.ds(start, size)
@@ -212,10 +213,13 @@
     wo_x.append(send_wo(0, 128, 128))
     wo_far = send_wo(d_far, 0, 256)
     wo_2 = send_wo(2, 0, 256)
-    s_wo = [send(op.at[:, cols(d)], Wo.at[col(d), wrow(blk)], partner) for d in range(NJ)]
+    s_wo = []
+    for d in range(NJ):
+        l_wo[d].wait_recv()
+        ref = Wo.at[col(d), wrow(blk)]
+        s_wo.append(send(ref, ref, partner))
     s_x = send(og.at[rows(zl * 2 + 1 - c)], X.at[blk], partner)
     l_x = local(og.at[rows(blk)], X.at[blk])
-    l_wo = [local(op.at[:, cols(d)], Wo.at[col(d), wrow(blk)]) for d in range(NJ)]
     l_prev = local(prev, gram_out)
     relay(0)
     own_far(0)
@@ -225,7 +229,6 @@
     pass_w2(2)
     rel_far(0)
     pass_w2(3)
-    l_wi.wait_recv()
     ref = Wi.at[x, :, :, c]
     d_wi[0] = send(ref, ref, partner)
     rel_far(1)
@@ -276,15 +279,11 @@
 
         lax.fori_loop(0, count, body, 0)
 
-    def compute_all(start, size):
-        def body(m, u):
-            block(start, size, [(x + 2 * m) % 4, (x + 2 * m + 1) % 4])
-            return u
-
-        lax.fori_loop(0, 2, body, 0)
+    def compute_pair(start, size, m):
+        block(start, size, [(x + 2 * m) % 4, (x + 2 * m + 1) % 4])
 
     l_x.wait_recv()
-    for cp in l_wo + [s_x] + s_wo:
+    for cp in [s_x] + s_wo:
         cp.wait_recv()
     arrived(0)
     d_wi[0].wait_recv()
@@ -360,19 +359,19 @@
     main = list(copies)
     r1 = add_up(0)
     compute(2 * ti, ti, d_near, 1, 1)
+    arrived(3)
+    lax.fori_loop(0, 2, lambda m, u: (compute_pair(3 * ti, ti, m), u)[1], 0)
+    r1b = add_up(1)
     r2, r3 = spread(0, r1)
     for cp in main:
         cp.wait_send()
     l_prev.wait_recv()
-    arrived(3)
-    compute_all(3 * ti, ti)
-    r1b = add_up(1)
+    r2b, r3b = spread(1, r1b)
     hand_over(0, r2, r3)
-    r2b, r3b = spread(1, r1b)
+    hand_over(1, r2b, r3b)
     for cp in copies:
-        if not cp.sent and cp not in r2b and cp not in r3b:
+        if not cp.sent:
             cp.wait_send()
-    hand_over(1, r2b, r3b)
     for cp in r3 + r3b:
         cp.wait_recv()
 

time: 58.9 us -> 56.1 us (0.952)
  Pallas kernels: 56.6 us -> 53.8 us
    pallas_call x1, Pallas kernels: 56.6 us -> 53.8 us  [local(): pl.pallas_call(kernel, out_shape=(jax.ShapeDtypeStruct((8, 128), F32), ja...]
where the time goes in v5:
time: 56.1 us; the launch traced here: 56 us
  Pallas kernels  53.8 us (96%)
  local copies, waits for them, and re-layouts  1.56 us (3%)
  between operations  0.64 us (1%)
    pallas_call x1, Pallas kernels, local(): pl.pallas_call(kernel, out_shape=(jax.ShapeDtypeStruct((8, 128), F32), ja...  53.8 us
    unnamed x2, local copies, waits for them, and re-layouts  1.56 us

profile of v5, /device:TPU:1, one launch (start us, length us, event | category | flops | bytes accessed | tf_op | source)
XLA Modules:
  0.0 56.0 jit_solution(18152026862672049535)
XLA Ops:
  0.6 53.8 %features_gram.1 = (f32[8,128]{1,0:T(8,128)S(1)}, f32[128,2048]{1,0:T(8,128)S(1)}) custom-call(bf16[4096,256]{1,0:T(8,128)(2,1)} %og.1, bf16[64,4096]{1,0:T(8,128)(2,1)} %bitcast.1, bf16[256,2048]{1,0:T(8,128)(2,1)} %op.1, bf16[64,2048]{1,0:T(8,128)(2,1)} %ip.1, f32[128,2048]{1,0:T(8,128)} %prev.1), custom_call_target="tpu_custom_call" | custom-call | tf_op jit(solution)/shard_map/features_gram/pallas_call | solution.py:414
  54.4 0.6 %copy.9 = f32[8,128]{1,0:T(8,128)} copy(f32[8,128]{1,0:T(8,128)S(1)} %get-tuple-element.4) | data formatting | bytes 8192
  55.0 1.0 %copy.10 = f32[128,2048]{1,0:T(8,128)} copy(f32[128,2048]{1,0:T(8,128)S(1)} %get-tuple-element.5) | data formatting | bytes 2097152

commit v6 on v5

--- a/solution.py
+++ b/solution.py
@@ -322,10 +322,10 @@
     d_wi[2].wait_recv()
     d_wo[2].wait_recv()
     pass_word(4)
-    compute(0, 2 * ti, 2, 1, 1)
     wo_near.wait_recv()
     ref = Wo.at[col(d_near), wrow(oblk)]
     d_wo.append(send(ref, ref, partner))
+    compute(0, 2 * ti, 2, 1, 1)
     compute(2 * ti, ti, 2, 1, 1)
     d_wo[3].wait_recv()
     me = dp * 2 + zl

time: 56.1 us -> 55 us (0.980)
  Pallas kernels: 53.8 us -> 52.7 us
    pallas_call x1, Pallas kernels: 53.8 us -> 52.7 us  [local(): pl.pallas_call(kernel, out_shape=(jax.ShapeDtypeStruct((8, 128), F32), ja...]
where the time goes in v6:
time: 55 us; the launch traced here: 54.9 us
  Pallas kernels  52.7 us (96%)
  local copies, waits for them, and re-layouts  1.56 us (3%)
  between operations  0.64 us (1%)
    pallas_call x1, Pallas kernels, local(): pl.pallas_call(kernel, out_shape=(jax.ShapeDtypeStruct((8, 128), F32), ja...  52.7 us
    unnamed x2, local copies, waits for them, and re-layouts  1.56 us

profile of v6, /device:TPU:1, one launch (start us, length us, event | category | flops | bytes accessed | tf_op | source)
XLA Modules:
  0.0 54.9 jit_solution(7950050345188710757)
XLA Ops:
  0.6 52.7 %features_gram.1 = (f32[8,128]{1,0:T(8,128)S(1)}, f32[128,2048]{1,0:T(8,128)S(1)}) custom-call(bf16[4096,256]{1,0:T(8,128)(2,1)} %og.1, bf16[64,4096]{1,0:T(8,128)(2,1)} %bitcast.1, bf16[256,2048]{1,0:T(8,128)(2,1)} %op.1, bf16[64,2048]{1,0:T(8,128)(2,1)} %ip.1, f32[128,2048]{1,0:T(8,128)} %prev.1), custom_call_target="tpu_custom_call" | custom-call | tf_op jit(solution)/shard_map/features_gram/pallas_call | solution.py:414
  53.3 0.6 %copy.9 = f32[8,128]{1,0:T(8,128)} copy(f32[8,128]{1,0:T(8,128)S(1)} %get-tuple-element.4) | data formatting | bytes 8192
  53.9 1.0 %copy.10 = f32[128,2048]{1,0:T(8,128)} copy(f32[128,2048]{1,0:T(8,128)S(1)} %get-tuple-element.5) | data formatting | bytes 2097152

commit v7 on v6

--- a/solution.py
+++ b/solution.py
@@ -343,13 +343,13 @@
         fall[clip, me, c] = own * F32(1.0 / math.sqrt(SEQ))
         mine = fall.at[clip, me, c]
         out = [send(mine, mine, plane(s)) for s in steps[::-1]][::-1]
-        both = [send(mine, mine, plane(s, 1 - c)) for s in steps[10:]] if clip else []
+        both = [send(mine, mine, plane(s, 1 - c)) for s in steps[4:]]
         return out, both + [send(mine, mine, partner)]
 
     def hand_over(clip, cps, out):
         for k, (s, cp) in enumerate(zip(steps, cps)):
             cp.wait_recv()
-            if clip and k >= 10:
+            if k >= 4:
                 continue
             x_, zh_, zl_ = shifted(*s, -1)
             ref = fall.at[clip, (x_ * 2 + zh_) * 2 + zl_, c]

time: 55 us -> 55.5 us (level)
  no operation moved by 1% of the time
where the time goes in v7:
time: 55.5 us; the launch traced here: 55.3 us
  Pallas kernels  53.1 us (96%)
  local copies, waits for them, and re-layouts  1.56 us (3%)
  between operations  0.64 us (1%)
    pallas_call x1, Pallas kernels, local(): pl.pallas_call(kernel, out_shape=(jax.ShapeDtypeStruct((8, 128), F32), ja...  53.1 us
    unnamed x2, local copies, waits for them, and re-layouts  1.56 us

profile of v7, /device:TPU:1, one launch (start us, length us, event | category | flops | bytes accessed | tf_op | source)
XLA Modules:
  0.0 55.3 jit_solution(6579865560061327717)
XLA Ops:
  0.6 53.1 %features_gram.1 = (f32[8,128]{1,0:T(8,128)S(1)}, f32[128,2048]{1,0:T(8,128)S(1)}) custom-call(bf16[4096,256]{1,0:T(8,128)(2,1)} %og.1, bf16[64,4096]{1,0:T(8,128)(2,1)} %bitcast.1, bf16[256,2048]{1,0:T(8,128)(2,1)} %op.1, bf16[64,2048]{1,0:T(8,128)(2,1)} %ip.1, f32[128,2048]{1,0:T(8,128)} %prev.1), custom_call_target="tpu_custom_call" | custom-call | tf_op jit(solution)/shard_map/features_gram/pallas_call | solution.py:414
  53.8 0.6 %copy.9 = f32[8,128]{1,0:T(8,128)} copy(f32[8,128]{1,0:T(8,128)S(1)} %get-tuple-element.4) | data formatting | bytes 8192
  54.4 1.0 %copy.10 = f32[128,2048]{1,0:T(8,128)} copy(f32[128,2048]{1,0:T(8,128)S(1)} %get-tuple-element.5) | data formatting | bytes 2097152
